TPU v7x, 256 devices: a whole 4x4x8 slice. The times are simulated.
256 devices in a mesh: rep: 16 (over x, y_hi, core), tp: 16 (over z, y_lo).
Axes of the slice: x: 4, y: 4 (y_hi: 2, y_lo: 2; y = y_hi * 2 + y_lo), z: 8, core: 2. Of those that a mesh axis runs over, the one named last changes fastest.
Arguments:
- queries: bfloat16 [64, 8192], P('rep', 'tp'), may hold values from -160 to 160
- assignment: int32 [64], replicated, may hold values from 0 to 63, each once
- prefix_keys: bfloat16 [131072, 1024], P(('rep', 'tp')), may hold values from -6 to 6
- prefix_values: bfloat16 [131072, 1024], P(('rep', 'tp')), may hold values from -6 to 6
- suffix_keys: bfloat16 [64, 2048, 1024], P('rep', 'tp'), may hold values from -10 to 10
- suffix_values: bfloat16 [64, 2048, 1024], P('rep', 'tp'), may hold values from -6 to 6
- lengths: int32 [64], P('rep'), may hold values from 1 to 2048, 65536 in all
Outputs:
- attended: bfloat16 [64, 8192], P('rep', 'tp')
Inputs may be any that keep to these rules, and one draw needn't show every extreme that they name: `assignment`: each request row names its own slot. `lengths`: some slot holds exactly 2048 live positions.
All inputs are finite; a program needn't handle non-finite values. No bound on the sum of `lengths` on one device may be relied on, other than what follows from the above.
Results may differ from a plain program's by a relative error of at most 0.0045.
Values may be sent and summed in bfloat16 or wider, within the bound.
A program may use at most 64 MiB of HBM per device.

v0:
```python
import functools
import math

import jax
import jax.numpy as jnp
from jax import lax
from jax.experimental import pallas as pl
from jax.experimental.pallas import tpu as pltpu
from jax.sharding import PartitionSpec as P

MESH = pl.DeviceIdType.MESH
HD = 128
HEADS_CORE = 4
C2 = math.log2(math.e) * HD ** (-0.5)
NEG = -(2.0**100)
BF = jnp.bfloat16
F32 = jnp.float32
NT = (((1,), (1,)), ((), ()))
NN = (((1,), (0,)), ((), ()))


def dot(a, b, dims):
    return lax.dot_general(a, b, dims, preferred_element_type=F32)


def kernel(
    q_hbm, asg_hbm, len_hbm, pk, pv, sk, sv, out_ref,
    kbuf, vbuf, skbuf, svbuf, qf, q0, q1, q2, qs, perm, lens, lensall, bias, sbuf, r1, s2, r2,
    q_ref, asg_ref, len_ref, smallsem, ldsem, xsend, xrecv, zsend, zrecv, gsend, grecv, rsend, rrecv, tsend, trecv,
):
    rep, tp = lax.axis_index("rep"), lax.axis_index("tp")
    x, yh, c = rep // 4, (rep // 2) % 2, rep % 2
    z, yl = tp // 2, tp % 2
    y = yh * 2 + yl
    hz = z // 4

    def dev(x_, y_, z_, c_):
        return (x_ * 4 + (y_ // 2) * 2 + c_, z_ * 2 + y_ % 2)

    small = [
        pltpu.make_async_copy(src, dst, smallsem.at[i])
        for i, (src, dst) in enumerate(((q_hbm, q_ref), (asg_hbm, asg_ref), (len_hbm, len_ref)))
    ]
    for copy in small:
        copy.start()

    mine = pl.multiple_of(c * 512, 512)
    theirs = pl.multiple_of((1 - c) * 512, 512)
    rows2 = pl.multiple_of(c * 512, 512)
    pairs = ((pk, kbuf), (sk, skbuf), (pv, vbuf), (sv, svbuf))

    def local_dst(i):
        buf = pairs[i][1]
        return buf.at[pl.ds(rows2, 512)] if i % 2 == 0 else buf.at[pl.ds(c * 4, 4)]

    def src_of(i, cols):
        ref = pairs[i][0]
        return ref.at[:, pl.ds(cols, 512)] if i % 2 == 0 else ref.at[:, :, pl.ds(cols, 512)]

    loads = [pltpu.make_async_copy(src_of(i, mine), local_dst(i), ldsem.at[i]) for i in range(4)]
    barrier = pltpu.get_barrier_semaphore()

    def greet(x_, y_, z_, c_):
        pl.semaphore_signal(barrier, inc=1, device_id=dev(x_, y_, z_, c_), device_id_type=MESH)

    partner = dev(x, y, z, 1 - c)
    for k in range(4):
        for cs in range(2):
            zs = 4 * c + k

            @pl.when(jnp.logical_or(zs != z, cs != c))
            def _(zs=zs, cs=cs):
                greet(x, y, zs, cs)

    greet(x, y, z, 1 - c)
    for o in range(1, 16):
        greet((x + o // 4) % 4, (y + o % 4) % 4, z, c)
    for zs in range(8):

        @pl.when(jnp.logical_or(jnp.logical_or(zs != z, z % 4 != y), hz != c))
        def _(zs=zs):
            greet(x, z % 4, zs, hz)

    for copy in loads:
        copy.start()

    small[0].wait()
    q = q_ref[...].astype(F32)
    for g in range(4):
        qf[g * 4 : g * 4 + 4, :] = q[:, g * 128 : (g + 1) * 128]
    q0[...] = qf[...].astype(BF)

    n_z = jnp.where(hz == c, 7, 8)
    n_t = jnp.where(4 * c + y == z, 7, 8)
    pl.semaphore_wait(barrier, 16 + n_z + n_t)

    def ztile(ref_z):
        return q1.at[ref_z % 4, pl.ds(pl.multiple_of(c * 16, 16), 16)]

    for o in (4, 3, 5, 2, 6, 1, 7):
        z_ = (z + o) % 8
        pltpu.make_async_remote_copy(
            src_ref=q0, dst_ref=ztile(z), send_sem=zsend.at[0], recv_sem=zrecv.at[z % 4],
            device_id=dev(x, y, z_, hz), device_id_type=MESH,
        ).start()

    @pl.when(hz == c)
    def _():
        pltpu.make_async_copy(q0, ztile(z), zrecv.at[z % 4]).start()

    @pl.when(hz != c)
    def _():
        pltpu.make_async_remote_copy(
            src_ref=q0, dst_ref=ztile(z), send_sem=zsend.at[1], recv_sem=zrecv.at[z % 4],
            device_id=partner, device_id_type=MESH,
        ).start()

    exchanges = [
        pltpu.make_async_remote_copy(
            src_ref=src_of(i, theirs), dst_ref=local_dst(i), send_sem=xsend.at[i], recv_sem=xrecv.at[i],
            device_id=partner, device_id_type=MESH,
        )
        for i in range(4)
    ]
    exchanges.append(
        pltpu.make_async_remote_copy(
            src_ref=lens, dst_ref=lensall, send_sem=xsend.at[4], recv_sem=xrecv.at[4],
            device_id=partner, device_id_type=MESH,
        )
    )
    exchanges[0].start()

    small[1].wait()
    small[2].wait()
    own_len = jnp.zeros((8, 128), jnp.int32)
    sub8 = lax.broadcasted_iota(jnp.int32, (8, 128), 0)
    for s in range(4):
        own_len = jnp.where(sub8 % 4 == s, len_ref[s], own_len)
    lens[...] = own_len

    exchanges[4].start()

    lane = lax.broadcasted_iota(jnp.int32, (1, 128), 1)
    lane_row = ((lane // 64) * 2 + (lane // 16) % 2) * 4 + lane % 4
    lane_g = ((lane // 32) % 2) * 4 + (lane // 4) % 4
    sub = lax.broadcasted_iota(jnp.int32, (512, 128), 0)
    sub_row = (sub // 128) * 16 + ((sub // 64) % 2) * 8 + ((sub // 16) % 2) * 4 + sub % 4
    sub_g = ((sub // 32) % 2) * 4 + (sub // 4) % 4
    sub_code = sub_row * 8 + sub_g
    for xs in range(4):
        held = jnp.zeros((1, 128), jnp.int32)
        for r in range(16):
            held = jnp.where(lane_row == r, asg_ref[xs * 16 + r], held)
        code = held * 8 + lane_g
        perm[:, xs * 128 : (xs + 1) * 128] = jnp.where(sub_code == code, 1.0, 0.0).astype(BF)

    me_rows = pl.ds(pl.multiple_of((x * 4 + y) * 32, 32), 32)
    for k in range(4):
        pltpu.make_async_copy(q1.at[k], q1.at[k], zrecv.at[k]).wait()
    for i in range(4):
        k = (y + 1 + i) % 4
        pltpu.make_async_copy(q1.at[k], q2.at[k, me_rows], grecv.at[k]).start()
        for o in range(1, 16):
            y_ = (y + o % 4) % 4
            k = (y_ + 1 + i) % 4
            pltpu.make_async_remote_copy(
                src_ref=q1.at[k], dst_ref=q2.at[k, me_rows], send_sem=gsend, recv_sem=grecv.at[k],
                device_id=dev((x + o // 4) % 4, y_, z, c), device_id_type=MESH,
            ).start()
        if i < 3:
            exchanges[(2, 1, 3)[i]].start()

    exchanges[4].wait_recv()
    rows = lax.broadcasted_iota(jnp.int32, (128, 128), 0)
    lanes = lax.broadcasted_iota(jnp.int32, (128, 128), 1)
    lens_own = jnp.concatenate([lens[...]] * 16, axis=0)
    lens_other = jnp.concatenate([lensall[...]] * 16, axis=0)
    row_c = (rows // 16) % 2
    live = jnp.where(row_c == c, lens_own, lens_other) - tp * 128
    live = jnp.where(rows // 64 == yh, live, 0)
    row_slot = row_c * 4 + rows % 4
    for s in range(8):
        limit = jnp.where(row_slot == s, live, 0)
        bias[:, s * 128 : s * 128 + 128] = jnp.where(lanes < limit, 0.0, NEG)

    for i in range(4):
        loads[i].wait()
        exchanges[i].wait_recv()

    eye = rows == lanes
    ones = jnp.ones((1024, 128), BF)
    stat_row = lax.broadcasted_iota(jnp.int32, (16, 128), 0)

    def as_row(column):
        return jnp.sum(jnp.where(eye, column, 0.0), axis=0, keepdims=True)

    def stat_tile(top, total):
        hi = total.astype(BF).astype(F32)
        return jnp.where(stat_row == 0, top, jnp.where(stat_row == 1, hi, total - hi)).astype(BF)

    def weights(scores, top):
        return jnp.exp2(scores - top).astype(BF)

    def largest(scores):
        return jnp.max(scores, axis=1, keepdims=True)

    def head(i, _):
        k = (y + 1 + i) % 4
        cols = pl.ds(pl.multiple_of(k * 128, 128), 128)
        pltpu.make_async_copy(q2.at[k], q2.at[k], grecv.at[k]).wait()
        qs[...] = dot(perm[...], q2[k], NN).astype(BF)
        chunks = [(x + 1 + a) % 4 for a in range(4)]
        parts = [qs[pl.ds(pl.multiple_of(j * 128, 128), 128), :] for j in chunks]
        keys = kbuf[:, cols]
        values = jnp.concatenate([vbuf[:, cols], ones], axis=1)
        suffix_keys = skbuf[:, :, cols].reshape(1024, 128)
        suffix_values = jnp.concatenate([svbuf[:, :, cols].reshape(1024, 128), ones], axis=1)

        s0 = dot(jnp.concatenate(parts[:2], axis=0), keys, NT) * C2
        s1 = dot(jnp.concatenate(parts[2:], axis=0), keys, NT) * C2
        ss = dot(parts[3], suffix_keys, NT) * C2 + bias[...]
        m0 = largest(s0).astype(BF).astype(F32)
        n0 = dot(weights(s0, m0), values, NN)
        m1 = largest(s1)
        m1 = jnp.concatenate([m1[:128], jnp.maximum(m1[128:], largest(ss))], axis=0).astype(BF).astype(F32)
        n1 = dot(weights(s1, m1), values, NN)
        ns = dot(weights(ss, m1[128:]), suffix_values, NN)

        pieces = [
            (m0[:128], n0[:128]),
            (m0[128:], n0[128:]),
            (m1[:128], n1[:128]),
            (m1[128:], n1[128:] + ns),
        ]
        for a in range(4):
            m, n = pieces[a]
            slot = i * 4 + a
            sbuf[slot, :128, :] = n[:, :128].astype(BF)
            sbuf[slot, 128:, :] = stat_tile(as_row(m), as_row(n[:, 128:]))

            def send(slot=slot, j=chunks[a]):
                pltpu.make_async_remote_copy(
                    src_ref=sbuf.at[slot], dst_ref=r1.at[x * 4 + y], send_sem=rsend, recv_sem=rrecv,
                    device_id=dev(j, k, z, c), device_id_type=MESH,
                ).start()

            if a < 3:
                send()
            else:
                pl.when(i < 3)(send)
        return 0

    lax.fori_loop(0, 4, head, 0)
    pltpu.make_async_copy(sbuf.at[15], r1.at[x * 4 + y], rrecv).start()

    pltpu.make_async_copy(r1, r1, rrecv).wait()
    stats = [r1[i, 128:, :].astype(F32) for i in range(16)]
    top = functools.reduce(jnp.maximum, [s[0:1] for s in stats])
    ws = [jnp.exp2(s[0:1] - top) for s in stats]
    total = functools.reduce(jnp.add, [w * (s[1:2] + s[2:3]) for w, s in zip(ws, stats)])
    his = [w.astype(BF).astype(F32) for w in ws]
    spread = [
        jnp.concatenate([jnp.where(eye, w, 0.0).astype(BF) for w in part], axis=1)
        for part in (his, [w - h for w, h in zip(ws, his)])
    ]
    both = dot(jnp.concatenate(spread, axis=0), jnp.concatenate([r1[i, :128, :] for i in range(16)], axis=0), NN)
    flat = (both[:128] + both[128:]).astype(BF)
    stat = stat_tile(top, total)
    for d in range(8):
        s2[d, :16, :] = flat[d * 16 : d * 16 + 16, :]
        s2[d, 16:, :] = stat

    zt = 4 * c + y
    for o in range(1, 8):
        y_, c_ = (y + o // 2) % 4, (c + o % 2) % 2
        pltpu.make_async_remote_copy(
            src_ref=s2.at[y_ * 2 + c_], dst_ref=r2.at[z], send_sem=tsend.at[0], recv_sem=trecv,
            device_id=dev(x, y_, zt, c_), device_id_type=MESH,
        ).start()

    @pl.when(zt == z)
    def _():
        pltpu.make_async_copy(s2.at[y * 2 + c], r2.at[z], trecv).start()

    @pl.when(zt != z)
    def _():
        pltpu.make_async_remote_copy(
            src_ref=s2.at[y * 2 + c], dst_ref=r2.at[z], send_sem=tsend.at[1], recv_sem=trecv,
            device_id=dev(x, y, zt, c), device_id_type=MESH,
        ).start()

    pltpu.make_async_copy(r2, r2, trecv).wait()

    offset = y * 32 + c * 16
    pick = lax.broadcasted_iota(jnp.int32, (16, 128), 1) == lax.broadcasted_iota(jnp.int32, (16, 128), 0) + offset
    stats = [r2[i, 16:, :].astype(F32) for i in range(8)]
    m2 = functools.reduce(jnp.maximum, [s[0:1] for s in stats])
    ws = [jnp.exp2(s[0:1] - m2) for s in stats]
    total = functools.reduce(jnp.add, [w * (s[1:2] + s[2:3]) for w, s in zip(ws, stats)])
    acc = jnp.zeros((16, 128), F32)
    for i in range(8):
        column = jnp.sum(jnp.where(pick, ws[i], 0.0), axis=1, keepdims=True)
        acc = acc + column * r2[i, :16, :].astype(F32)
    column = jnp.sum(jnp.where(pick, total, 0.0), axis=1, keepdims=True)
    acc = acc / column
    for g in range(4):
        out_ref[:, g * 128 : (g + 1) * 128] = acc[g * 4 : g * 4 + 4, :].astype(BF)

    for i in range(5):
        exchanges[i].wait_send()
    pltpu.make_async_copy(s2.at[pl.ds(0, 7), pl.ds(0, 16)], s2.at[pl.ds(0, 7), pl.ds(0, 16)], zsend.at[0]).wait()

    @pl.when(hz != c)
    def _():
        pltpu.make_async_copy(q0, q0, zsend.at[1]).wait()

    most = q2.at[:, pl.ds(0, 480)]
    pltpu.make_async_copy(most, most, gsend).wait()
    most = sbuf.at[pl.ds(0, 15)]
    pltpu.make_async_copy(most, most, rsend).wait()
    most = s2.at[pl.ds(0, 7)]
    pltpu.make_async_copy(most, most, tsend.at[0]).wait()

    @pl.when(zt != z)
    def _():
        pltpu.make_async_copy(s2.at[0], s2.at[0], tsend.at[1]).wait()


def shards(queries, assignment, prefix_keys, prefix_values, suffix_keys, suffix_values, lengths):
    vmem, far = pl.BlockSpec(memory_space=pltpu.VMEM), pl.BlockSpec(memory_space=pl.ANY)
    dma = pltpu.SemaphoreType.DMA
    return pl.pallas_call(
        kernel,
        out_shape=jax.ShapeDtypeStruct(queries.shape, BF),
        in_specs=[far, far, far, far, far, far, far],
        out_specs=vmem,
        scratch_shapes=[
            pltpu.VMEM((1024, 512), BF),
            pltpu.VMEM((1024, 512), BF),
            pltpu.VMEM((8, 128, 512), BF),
            pltpu.VMEM((8, 128, 512), BF),
            pltpu.VMEM((16, 128), F32),
            pltpu.VMEM((16, 128), BF),
            pltpu.VMEM((4, 32, 128), BF),
            pltpu.VMEM((4, 512, 128), BF),
            pltpu.VMEM((512, 128), BF),
            pltpu.VMEM((512, 512), BF),
            pltpu.VMEM((8, 128), jnp.int32),
            pltpu.VMEM((8, 128), jnp.int32),
            pltpu.VMEM((128, 1024), F32),
            pltpu.VMEM((16, 144, 128), BF),
            pltpu.VMEM((16, 144, 128), BF),
            pltpu.VMEM((8, 32, 128), BF),
            pltpu.VMEM((8, 32, 128), BF),
            pltpu.VMEM((4, 512), BF),
            pltpu.SMEM((64,), jnp.int32),
            pltpu.SMEM((4,), jnp.int32),
            dma((3,)),
            dma((4,)),
            dma((5,)),
            dma((5,)),
            dma((2,)),
            dma((4,)),
            dma(()),
            dma((4,)),
            dma(()),
            dma(()),
            dma((2,)),
            dma(()),
        ],
        compiler_params=pltpu.CompilerParams(
            collective_id=0, has_side_effects=True, vmem_limit_bytes=48 * 1024 * 1024
        ),
        cost_estimate=pl.CostEstimate(flops=1_300_000_000, bytes_accessed=4_300_000, transcendentals=2_600_000),
    )(
        *(
            pltpu.with_memory_space_constraint(operand, pltpu.HBM)
            for operand in (
                queries, assignment, lengths, prefix_keys, prefix_values, suffix_keys, suffix_values
            )
        )
    )


def solution(mesh):
    in_specs = (
        P("rep", "tp"),
        P(),
        P(("rep", "tp"), None),
        P(("rep", "tp"), None),
        P("rep", "tp", None),
        P("rep", "tp", None),
        P("rep"),
    )
    out_specs = P("rep", "tp")
    return jax.shard_map(shards, mesh=mesh, in_specs=in_specs, out_specs=out_specs, check_vma=False)
```

profile of v0, /device:TPU:25, one launch (start us, length us, event | category | flops | bytes accessed | tf_op | source)
XLA Modules:
  0.0 37.0 jit_solution(18102164614619023373)
XLA Ops:
  0.0 36.4 %shard_map.73 = bf16[4,512]{1,0:T(4,128)(2,1)S(1)} custom-call(bf16[4,512]{1,0:T(4,128)(2,1)} %q_hbm.1, s32[64]{0:T(128)} %asg_hbm.1, s32[4]{0:T(128)} %len_hbm.1, bf16[512,1024]{1,0:T(8,128)(2,1)} %pk.1, bf16[512,1024]{1,0:T(8,128)(2,1)} %pv.1, bf16[4,128,1024]{2,1,0:T(8,128)(2,1)} %sk.1, bf16[4,128,1024]{2,1,0:T(8,128)(2,1)} %sv.1), custom_call_target="tpu_custom_call" | custom-call | flops 1300000000 | bytes 4300000 | tf_op jit(solution)/shard_map/pallas_call | solution.py:332
  36.4 0.6 %copy.9 = bf16[4,512]{1,0:T(4,128)(2,1)} copy(bf16[4,512]{1,0:T(4,128)(2,1)S(1)} %shard_map.73) | data formatting | bytes 8192
where the time goes:
time: 37.5 us; the launch traced here: 37 us
  Pallas kernels  36.4 us (97%)
  local copies, waits for them, and re-layouts  0.6 us (2%)
    pallas_call x1, Pallas kernels, shards(): pl.pallas_call(kernel, out_shape=jax.ShapeDtypeStruct(queries.shape, BF),...  36.4 us

commit v1 on v0

--- a/solution.py
+++ b/solution.py
@@ -171,13 +171,12 @@
             exchanges[(2, 1, 3)[i]].start()
 
     exchanges[4].wait_recv()
-    rows = lax.broadcasted_iota(jnp.int32, (128, 128), 0)
-    lanes = lax.broadcasted_iota(jnp.int32, (128, 128), 1)
-    lens_own = jnp.concatenate([lens[...]] * 16, axis=0)
-    lens_other = jnp.concatenate([lensall[...]] * 16, axis=0)
+    rows = lax.broadcasted_iota(jnp.int32, (64, 128), 0)
+    lanes = lax.broadcasted_iota(jnp.int32, (64, 128), 1)
+    lens_own = jnp.concatenate([lens[...]] * 8, axis=0)
+    lens_other = jnp.concatenate([lensall[...]] * 8, axis=0)
     row_c = (rows // 16) % 2
     live = jnp.where(row_c == c, lens_own, lens_other) - tp * 128
-    live = jnp.where(rows // 64 == yh, live, 0)
     row_slot = row_c * 4 + rows % 4
     for s in range(8):
         limit = jnp.where(row_slot == s, live, 0)
@@ -187,7 +186,8 @@
         loads[i].wait()
         exchanges[i].wait_recv()
 
-    eye = rows == lanes
+    square = (128, 128)
+    eye = lax.broadcasted_iota(jnp.int32, square, 0) == lax.broadcasted_iota(jnp.int32, square, 1)
     ones = jnp.ones((1024, 128), BF)
     stat_row = lax.broadcasted_iota(jnp.int32, (16, 128), 0)
 
@@ -218,36 +218,37 @@
 
         s0 = dot(jnp.concatenate(parts[:2], axis=0), keys, NT) * C2
         s1 = dot(jnp.concatenate(parts[2:], axis=0), keys, NT) * C2
-        ss = dot(parts[3], suffix_keys, NT) * C2 + bias[...]
+        own = pl.ds(pl.multiple_of(x * 128 + yh * 64, 64), 64)
+        ss = dot(qs[own, :], suffix_keys, NT) * C2 + bias[...]
+
+        def send(a):
+            pltpu.make_async_remote_copy(
+                src_ref=sbuf.at[i * 4 + a], dst_ref=r1.at[x * 4 + y], send_sem=rsend, recv_sem=rrecv,
+                device_id=dev(chunks[a], k, z, c), device_id_type=MESH,
+            ).start()
+
+        def put(a, m, n):
+            sbuf[i * 4 + a, :128, :] = n[:, :128].astype(BF)
+            sbuf[i * 4 + a, 128:, :] = stat_tile(as_row(m), as_row(n[:, 128:]))
+
         m0 = largest(s0).astype(BF).astype(F32)
         n0 = dot(weights(s0, m0), values, NN)
-        m1 = largest(s1)
-        m1 = jnp.concatenate([m1[:128], jnp.maximum(m1[128:], largest(ss))], axis=0).astype(BF).astype(F32)
+        put(0, m0[:128], n0[:128])
+        send(0)
+        put(1, m0[128:], n0[128:])
+        send(1)
+
+        m1, ms = largest(s1), largest(ss)
+        low = jnp.full((64, 1), NEG, F32)
+        ms = jnp.concatenate([jnp.where(yh == 0, ms, low), jnp.where(yh == 0, low, ms)], axis=0)
+        m1 = jnp.concatenate([m1[:128], jnp.maximum(m1[128:], ms)], axis=0).astype(BF).astype(F32)
         n1 = dot(weights(s1, m1), values, NN)
-        ns = dot(weights(ss, m1[128:]), suffix_values, NN)
-
-        pieces = [
-            (m0[:128], n0[:128]),
-            (m0[128:], n0[128:]),
-            (m1[:128], n1[:128]),
-            (m1[128:], n1[128:] + ns),
-        ]
-        for a in range(4):
-            m, n = pieces[a]
-            slot = i * 4 + a
-            sbuf[slot, :128, :] = n[:, :128].astype(BF)
-            sbuf[slot, 128:, :] = stat_tile(as_row(m), as_row(n[:, 128:]))
-
-            def send(slot=slot, j=chunks[a]):
-                pltpu.make_async_remote_copy(
-                    src_ref=sbuf.at[slot], dst_ref=r1.at[x * 4 + y], send_sem=rsend, recv_sem=rrecv,
-                    device_id=dev(j, k, z, c), device_id_type=MESH,
-                ).start()
-
-            if a < 3:
-                send()
-            else:
-                pl.when(i < 3)(send)
+        ns = dot(weights(ss, jnp.where(yh == 0, m1[128:192], m1[192:])), suffix_values, NN)
+        ns = jnp.concatenate([jnp.where(yh == 0, ns, 0.0), jnp.where(yh == 0, 0.0, ns)], axis=0)
+        put(2, m1[:128], n1[:128])
+        send(2)
+        put(3, m1[128:], n1[128:] + ns)
+        pl.when(i < 3)(lambda: send(3))
         return 0
 
     lax.fori_loop(0, 4, head, 0)
@@ -347,7 +348,7 @@
             pltpu.VMEM((512, 512), BF),
             pltpu.VMEM((8, 128), jnp.int32),
             pltpu.VMEM((8, 128), jnp.int32),
-            pltpu.VMEM((128, 1024), F32),
+            pltpu.VMEM((64, 1024), F32),
             pltpu.VMEM((16, 144, 128), BF),
             pltpu.VMEM((16, 144, 128), BF),
             pltpu.VMEM((8, 32, 128), BF),

time: 37.5 us -> 37.2 us (level)
  Pallas kernels: 36.4 us -> 36 us
    pallas_call x1, Pallas kernels: 36.4 us -> 36 us  [shards(): pl.pallas_call(kernel, out_shape=jax.ShapeDtypeStruct(queries.shape, BF),...]
where the time goes in v1:
time: 37.2 us; the launch traced here: 36.6 us
  Pallas kernels  36 us (97%)
  local copies, waits for them, and re-layouts  0.6 us (2%)
    pallas_call x1, Pallas kernels, shards(): pl.pallas_call(kernel, out_shape=jax.ShapeDtypeStruct(queries.shape, BF),...  36 us

profile of v1, /device:TPU:25, one launch (start us, length us, event | category | flops | bytes accessed | tf_op | source)
XLA Modules:
  0.0 36.6 jit_solution(12814510356788189134)
XLA Ops:
  0.0 36.0 %shard_map.73 = bf16[4,512]{1,0:T(4,128)(2,1)S(1)} custom-call(bf16[4,512]{1,0:T(4,128)(2,1)} %q_hbm.1, s32[64]{0:T(128)} %asg_hbm.1, s32[4]{0:T(128)} %len_hbm.1, bf16[512,1024]{1,0:T(8,128)(2,1)} %pk.1, bf16[512,1024]{1,0:T(8,128)(2,1)} %pv.1, bf16[4,128,1024]{2,1,0:T(8,128)(2,1)} %sk.1, bf16[4,128,1024]{2,1,0:T(8,128)(2,1)} %sv.1), custom_call_target="tpu_custom_call" | custom-call | flops 1300000000 | bytes 4300000 | tf_op jit(solution)/shard_map/pallas_call | solution.py:333
  36.1 0.6 %copy.9 = bf16[4,512]{1,0:T(4,128)(2,1)} copy(bf16[4,512]{1,0:T(4,128)(2,1)S(1)} %shard_map.73) | data formatting | bytes 8192

commit v2 on v1

--- a/solution.py
+++ b/solution.py
@@ -17,6 +17,9 @@
 F32 = jnp.float32
 NT = (((1,), (1,)), ((), ()))
 NN = (((1,), (0,)), ((), ()))
+AROUND = (
+    (1, 0), (3, 0), (0, 1), (0, 3), (2, 0), (1, 1), (3, 1), (2, 1), (0, 2), (1, 2), (3, 2), (2, 2), (1, 3), (3, 3), (2, 3),
+)
 
 
 def dot(a, b, dims):
@@ -33,6 +36,9 @@
     z, yl = tp // 2, tp % 2
     y = yh * 2 + yl
     hz = z // 4
+
+    def head_at(y_, i):
+        return (y_ + 1 + i + c * (2 - 2 * i)) % 4
 
     def dev(x_, y_, z_, c_):
         return (x_ * 4 + (y_ // 2) * 2 + c_, z_ * 2 + y_ % 2)
@@ -158,14 +164,14 @@
     for k in range(4):
         pltpu.make_async_copy(q1.at[k], q1.at[k], zrecv.at[k]).wait()
     for i in range(4):
-        k = (y + 1 + i) % 4
+        k = head_at(y, i)
         pltpu.make_async_copy(q1.at[k], q2.at[k, me_rows], grecv.at[k]).start()
-        for o in range(1, 16):
-            y_ = (y + o % 4) % 4
-            k = (y_ + 1 + i) % 4
+        for dx, dy in AROUND:
+            y_ = (y + dy) % 4
+            k = head_at(y_, i)
             pltpu.make_async_remote_copy(
                 src_ref=q1.at[k], dst_ref=q2.at[k, me_rows], send_sem=gsend, recv_sem=grecv.at[k],
-                device_id=dev((x + o // 4) % 4, y_, z, c), device_id_type=MESH,
+                device_id=dev((x + dx) % 4, y_, z, c), device_id_type=MESH,
             ).start()
         if i < 3:
             exchanges[(2, 1, 3)[i]].start()
@@ -205,11 +211,11 @@
         return jnp.max(scores, axis=1, keepdims=True)
 
     def head(i, _):
-        k = (y + 1 + i) % 4
+        k = head_at(y, i)
         cols = pl.ds(pl.multiple_of(k * 128, 128), 128)
         pltpu.make_async_copy(q2.at[k], q2.at[k], grecv.at[k]).wait()
         qs[...] = dot(perm[...], q2[k], NN).astype(BF)
-        chunks = [(x + 1 + a) % 4 for a in range(4)]
+        chunks = [(x + a) % 4 for a in (1, 3, 2, 0)]
         parts = [qs[pl.ds(pl.multiple_of(j * 128, 128), 128), :] for j in chunks]
         keys = kbuf[:, cols]
         values = jnp.concatenate([vbuf[:, cols], ones], axis=1)

time: 37.2 us -> 37.4 us (level); the launches traced: 36.6 us -> 37.3 us
  Pallas kernels: 36 us -> 36.7 us
    pallas_call x1, Pallas kernels: 36 us -> 36.7 us  [shards(): pl.pallas_call(kernel, out_shape=jax.ShapeDtypeStruct(queries.shape, BF),...]
where the time goes in v2:
time: 37.4 us; the launch traced here: 37.3 us
  Pallas kernels  36.7 us (98%)
  local copies, waits for them, and re-layouts  0.6 us (2%)
    pallas_call x1, Pallas kernels, shards(): pl.pallas_call(kernel, out_shape=jax.ShapeDtypeStruct(queries.shape, BF),...  36.7 us

profile of v2, /device:TPU:25, one launch (start us, length us, event | category | flops | bytes accessed | tf_op | source)
XLA Modules:
  0.0 37.3 jit_solution(10482810132628090860)
XLA Ops:
  0.0 36.7 %shard_map.73 = bf16[4,512]{1,0:T(4,128)(2,1)S(1)} custom-call(bf16[4,512]{1,0:T(4,128)(2,1)} %q_hbm.1, s32[64]{0:T(128)} %asg_hbm.1, s32[4]{0:T(128)} %len_hbm.1, bf16[512,1024]{1,0:T(8,128)(2,1)} %pk.1, bf16[512,1024]{1,0:T(8,128)(2,1)} %pv.1, bf16[4,128,1024]{2,1,0:T(8,128)(2,1)} %sk.1, bf16[4,128,1024]{2,1,0:T(8,128)(2,1)} %sv.1), custom_call_target="tpu_custom_call" | custom-call | flops 1300000000 | bytes 4300000 | tf_op jit(solution)/shard_map/pallas_call | solution.py:339
  36.7 0.6 %copy.9 = bf16[4,512]{1,0:T(4,128)(2,1)} copy(bf16[4,512]{1,0:T(4,128)(2,1)S(1)} %shard_map.73) | data formatting | bytes 8192

commit v3 on v2

--- a/solution.py
+++ b/solution.py
@@ -1,5 +1,4 @@
 import functools
-import math
 
 import jax
 import jax.numpy as jnp
@@ -11,7 +10,7 @@
 MESH = pl.DeviceIdType.MESH
 HD = 128
 HEADS_CORE = 4
-C2 = math.log2(math.e) * HD ** (-0.5)
+SCALE = HD ** (-0.5)
 NEG = -(2.0**100)
 BF = jnp.bfloat16
 F32 = jnp.float32
@@ -141,17 +140,17 @@
     own_len = jnp.zeros((8, 128), jnp.int32)
     sub8 = lax.broadcasted_iota(jnp.int32, (8, 128), 0)
     for s in range(4):
-        own_len = jnp.where(sub8 % 4 == s, len_ref[s], own_len)
+        own_len = jnp.where((sub8 & 3) == s, len_ref[s], own_len)
     lens[...] = own_len
 
     exchanges[4].start()
 
     lane = lax.broadcasted_iota(jnp.int32, (1, 128), 1)
-    lane_row = ((lane // 64) * 2 + (lane // 16) % 2) * 4 + lane % 4
-    lane_g = ((lane // 32) % 2) * 4 + (lane // 4) % 4
+    lane_row = ((lane >> 6) * 2 + ((lane >> 4) & 1)) * 4 + (lane & 3)
+    lane_g = ((lane >> 5) & 1) * 4 + ((lane >> 2) & 3)
     sub = lax.broadcasted_iota(jnp.int32, (512, 128), 0)
-    sub_row = (sub // 128) * 16 + ((sub // 64) % 2) * 8 + ((sub // 16) % 2) * 4 + sub % 4
-    sub_g = ((sub // 32) % 2) * 4 + (sub // 4) % 4
+    sub_row = (sub >> 6) * 8 + ((sub >> 4) & 1) * 4 + (sub & 3)
+    sub_g = ((sub >> 5) & 1) * 4 + ((sub >> 2) & 3)
     sub_code = sub_row * 8 + sub_g
     for xs in range(4):
         held = jnp.zeros((1, 128), jnp.int32)
@@ -181,9 +180,9 @@
     lanes = lax.broadcasted_iota(jnp.int32, (64, 128), 1)
     lens_own = jnp.concatenate([lens[...]] * 8, axis=0)
     lens_other = jnp.concatenate([lensall[...]] * 8, axis=0)
-    row_c = (rows // 16) % 2
+    row_c = (rows >> 4) & 1
     live = jnp.where(row_c == c, lens_own, lens_other) - tp * 128
-    row_slot = row_c * 4 + rows % 4
+    row_slot = row_c * 4 + (rows & 3)
     for s in range(8):
         limit = jnp.where(row_slot == s, live, 0)
         bias[:, s * 128 : s * 128 + 128] = jnp.where(lanes < limit, 0.0, NEG)
@@ -205,7 +204,7 @@
         return jnp.where(stat_row == 0, top, jnp.where(stat_row == 1, hi, total - hi)).astype(BF)
 
     def weights(scores, top):
-        return jnp.exp2(scores - top).astype(BF)
+        return jnp.exp(scores - top).astype(BF)
 
     def largest(scores):
         return jnp.max(scores, axis=1, keepdims=True)
@@ -222,10 +221,10 @@
         suffix_keys = skbuf[:, :, cols].reshape(1024, 128)
         suffix_values = jnp.concatenate([svbuf[:, :, cols].reshape(1024, 128), ones], axis=1)
 
-        s0 = dot(jnp.concatenate(parts[:2], axis=0), keys, NT) * C2
-        s1 = dot(jnp.concatenate(parts[2:], axis=0), keys, NT) * C2
+        s0 = dot(jnp.concatenate(parts[:2], axis=0), keys, NT) * SCALE
+        s1 = dot(jnp.concatenate(parts[2:], axis=0), keys, NT) * SCALE
         own = pl.ds(pl.multiple_of(x * 128 + yh * 64, 64), 64)
-        ss = dot(qs[own, :], suffix_keys, NT) * C2 + bias[...]
+        ss = dot(qs[own, :], suffix_keys, NT) * SCALE + bias[...]
 
         def send(a):
             pltpu.make_async_remote_copy(
@@ -263,7 +262,7 @@
     pltpu.make_async_copy(r1, r1, rrecv).wait()
     stats = [r1[i, 128:, :].astype(F32) for i in range(16)]
     top = functools.reduce(jnp.maximum, [s[0:1] for s in stats])
-    ws = [jnp.exp2(s[0:1] - top) for s in stats]
+    ws = [jnp.exp(s[0:1] - top) for s in stats]
     total = functools.reduce(jnp.add, [w * (s[1:2] + s[2:3]) for w, s in zip(ws, stats)])
     his = [w.astype(BF).astype(F32) for w in ws]
     spread = [
@@ -302,7 +301,7 @@
     pick = lax.broadcasted_iota(jnp.int32, (16, 128), 1) == lax.broadcasted_iota(jnp.int32, (16, 128), 0) + offset
     stats = [r2[i, 16:, :].astype(F32) for i in range(8)]
     m2 = functools.reduce(jnp.maximum, [s[0:1] for s in stats])
-    ws = [jnp.exp2(s[0:1] - m2) for s in stats]
+    ws = [jnp.exp(s[0:1] - m2) for s in stats]
     total = functools.reduce(jnp.add, [w * (s[1:2] + s[2:3]) for w, s in zip(ws, stats)])
     acc = jnp.zeros((16, 128), F32)
     for i in range(8):

time: 37.4 us -> 37.4 us (level)
  no operation moved by 1% of the time
where the time goes in v3:
time: 37.4 us; the launch traced here: 37.3 us
  Pallas kernels  36.7 us (98%)
  local copies, waits for them, and re-layouts  0.6 us (2%)
    pallas_call x1, Pallas kernels, shards(): pl.pallas_call(kernel, out_shape=jax.ShapeDtypeStruct(queries.shape, BF),...  36.7 us

profile of v3, /device:TPU:25, one launch (start us, length us, event | category | flops | bytes accessed | tf_op | source)
XLA Modules:
  0.0 37.3 jit_solution(18430231596033175862)
XLA Ops:
  0.0 36.7 %shard_map.73 = bf16[4,512]{1,0:T(4,128)(2,1)S(1)} custom-call(bf16[4,512]{1,0:T(4,128)(2,1)} %q_hbm.1, s32[64]{0:T(128)} %asg_hbm.1, s32[4]{0:T(128)} %len_hbm.1, bf16[512,1024]{1,0:T(8,128)(2,1)} %pk.1, bf16[512,1024]{1,0:T(8,128)(2,1)} %pv.1, bf16[4,128,1024]{2,1,0:T(8,128)(2,1)} %sk.1, bf16[4,128,1024]{2,1,0:T(8,128)(2,1)} %sv.1), custom_call_target="tpu_custom_call" | custom-call | flops 1300000000 | bytes 4300000 | tf_op jit(solution)/shard_map/pallas_call | solution.py:338
  36.7 0.6 %copy.9 = bf16[4,512]{1,0:T(4,128)(2,1)} copy(bf16[4,512]{1,0:T(4,128)(2,1)S(1)} %shard_map.73) | data formatting | bytes 8192

commit v4 on v3

--- a/solution.py
+++ b/solution.py
@@ -158,6 +158,10 @@
             held = jnp.where(lane_row == r, asg_ref[xs * 16 + r], held)
         code = held * 8 + lane_g
         perm[:, xs * 128 : (xs + 1) * 128] = jnp.where(sub_code == code, 1.0, 0.0).astype(BF)
+
+    @pl.when(c == 1)
+    def _():
+        exchanges[0].wait_recv()
 
     me_rows = pl.ds(pl.multiple_of((x * 4 + y) * 32, 32), 32)
     for k in range(4):
@@ -187,9 +191,14 @@
         limit = jnp.where(row_slot == s, live, 0)
         bias[:, s * 128 : s * 128 + 128] = jnp.where(lanes < limit, 0.0, NEG)
 
+    @pl.when(c == 0)
+    def _():
+        exchanges[0].wait_recv()
+
     for i in range(4):
         loads[i].wait()
-        exchanges[i].wait_recv()
+        if i > 0:
+            exchanges[i].wait_recv()
 
     square = (128, 128)
     eye = lax.broadcasted_iota(jnp.int32, square, 0) == lax.broadcasted_iota(jnp.int32, square, 1)

time: 37.4 us -> 37.4 us (level)
  no operation moved by 1% of the time
where the time goes in v4:
time: 37.4 us; the launch traced here: 37.3 us
  Pallas kernels  36.7 us (98%)
  local copies, waits for them, and re-layouts  0.6 us (2%)
    pallas_call x1, Pallas kernels, shards(): pl.pallas_call(kernel, out_shape=jax.ShapeDtypeStruct(queries.shape, BF),...  36.7 us

profile of v4, /device:TPU:25, one launch (start us, length us, event | category | flops | bytes accessed | tf_op | source)
XLA Modules:
  0.0 37.3 jit_solution(12375514298791059074)
XLA Ops:
  0.0 36.7 %shard_map.73 = bf16[4,512]{1,0:T(4,128)(2,1)S(1)} custom-call(bf16[4,512]{1,0:T(4,128)(2,1)} %q_hbm.1, s32[64]{0:T(128)} %asg_hbm.1, s32[4]{0:T(128)} %len_hbm.1, bf16[512,1024]{1,0:T(8,128)(2,1)} %pk.1, bf16[512,1024]{1,0:T(8,128)(2,1)} %pv.1, bf16[4,128,1024]{2,1,0:T(8,128)(2,1)} %sk.1, bf16[4,128,1024]{2,1,0:T(8,128)(2,1)} %sv.1), custom_call_target="tpu_custom_call" | custom-call | flops 1300000000 | bytes 4300000 | tf_op jit(solution)/shard_map/pallas_call | solution.py:347
  36.7 0.6 %copy.9 = bf16[4,512]{1,0:T(4,128)(2,1)} copy(bf16[4,512]{1,0:T(4,128)(2,1)S(1)} %shard_map.73) | data formatting | bytes 8192

commit v5 on v4

--- a/solution.py
+++ b/solution.py
@@ -37,7 +37,7 @@
     hz = z // 4
 
     def head_at(y_, i):
-        return (y_ + 1 + i + c * (2 - 2 * i)) % 4
+        return (c * (y_ + 3 - i) + (1 - c) * i) % 4
 
     def dev(x_, y_, z_, c_):
         return (x_ * 4 + (y_ // 2) * 2 + c_, z_ * 2 + y_ % 2)
@@ -262,11 +262,15 @@
         put(2, m1[:128], n1[:128])
         send(2)
         put(3, m1[128:], n1[128:] + ns)
-        pl.when(i < 3)(lambda: send(3))
+        pl.when(k != y)(lambda: send(3))
+
+        @pl.when(k == y)
+        def _():
+            pltpu.make_async_copy(sbuf.at[i * 4 + 3], r1.at[x * 4 + y], rrecv).start()
+
         return 0
 
     lax.fori_loop(0, 4, head, 0)
-    pltpu.make_async_copy(sbuf.at[15], r1.at[x * 4 + y], rrecv).start()
 
     pltpu.make_async_copy(r1, r1, rrecv).wait()
     stats = [r1[i, 128:, :].astype(F32) for i in range(16)]

time: 37.4 us -> 37.5 us (level)
  no operation moved by 1% of the time
where the time goes in v5:
time: 37.5 us; the launch traced here: 37.4 us
  Pallas kernels  36.8 us (98%)
  local copies, waits for them, and re-layouts  0.6 us (2%)
    pallas_call x1, Pallas kernels, shards(): pl.pallas_call(kernel, out_shape=jax.ShapeDtypeStruct(queries.shape, BF),...  36.8 us

profile of v5, /device:TPU:25, one launch (start us, length us, event | category | flops | bytes accessed | tf_op | source)
XLA Modules:
  0.0 37.4 jit_solution(8834168098758784322)
XLA Ops:
  0.0 36.8 %shard_map.73 = bf16[4,512]{1,0:T(4,128)(2,1)S(1)} custom-call(bf16[4,512]{1,0:T(4,128)(2,1)} %q_hbm.1, s32[64]{0:T(128)} %asg_hbm.1, s32[4]{0:T(128)} %len_hbm.1, bf16[512,1024]{1,0:T(8,128)(2,1)} %pk.1, bf16[512,1024]{1,0:T(8,128)(2,1)} %pv.1, bf16[4,128,1024]{2,1,0:T(8,128)(2,1)} %sk.1, bf16[4,128,1024]{2,1,0:T(8,128)(2,1)} %sv.1), custom_call_target="tpu_custom_call" | custom-call | flops 1300000000 | bytes 4300000 | tf_op jit(solution)/shard_map/pallas_call | solution.py:351
  36.8 0.6 %copy.9 = bf16[4,512]{1,0:T(4,128)(2,1)} copy(bf16[4,512]{1,0:T(4,128)(2,1)S(1)} %shard_map.73) | data formatting | bytes 8192

commit v6 on v3

--- a/solution.py
+++ b/solution.py
@@ -86,9 +86,6 @@
         def _(zs=zs):
             greet(x, z % 4, zs, hz)
 
-    for copy in loads:
-        copy.start()
-
     small[0].wait()
     q = q_ref[...].astype(F32)
     for g in range(4):
@@ -134,6 +131,8 @@
         )
     )
     exchanges[0].start()
+    for copy in loads:
+        copy.start()
 
     small[1].wait()
     small[2].wait()

time: 37.4 us -> 37.4 us (level)
  no operation moved by 1% of the time
where the time goes in v6:
time: 37.4 us; the launch traced here: 37.3 us
  Pallas kernels  36.7 us (98%)
  local copies, waits for them, and re-layouts  0.6 us (2%)
    pallas_call x1, Pallas kernels, shards(): pl.pallas_call(kernel, out_shape=jax.ShapeDtypeStruct(queries.shape, BF),...  36.7 us

profile of v6, /device:TPU:25, one launch (start us, length us, event | category | flops | bytes accessed | tf_op | source)
XLA Modules:
  0.0 37.3 jit_solution(10274911546835591918)
XLA Ops:
  0.0 36.7 %shard_map.73 = bf16[4,512]{1,0:T(4,128)(2,1)S(1)} custom-call(bf16[4,512]{1,0:T(4,128)(2,1)} %q_hbm.1, s32[64]{0:T(128)} %asg_hbm.1, s32[4]{0:T(128)} %len_hbm.1, bf16[512,1024]{1,0:T(8,128)(2,1)} %pk.1, bf16[512,1024]{1,0:T(8,128)(2,1)} %pv.1, bf16[4,128,1024]{2,1,0:T(8,128)(2,1)} %sk.1, bf16[4,128,1024]{2,1,0:T(8,128)(2,1)} %sv.1), custom_call_target="tpu_custom_call" | custom-call | flops 1300000000 | bytes 4300000 | tf_op jit(solution)/shard_map/pallas_call | solution.py:337
  36.7 0.6 %copy.9 = bf16[4,512]{1,0:T(4,128)(2,1)} copy(bf16[4,512]{1,0:T(4,128)(2,1)S(1)} %shard_map.73) | data formatting | bytes 8192
